TPU v7x, 512 devices: a whole 4x8x8 slice. The times are simulated.
512 devices in a mesh: lon: 64 (over x, z, y_hi), lat: 8 (over y_lo, core).
Axes of the slice: x: 4, y: 8 (y_hi: 2, y_lo: 4; y = y_hi * 4 + y_lo), z: 8, core: 2. Of those that a mesh axis runs over, the one named last changes fastest.
Arguments:
- fields: bfloat16 [128, 2880, 640], P('lat', 'lon'), may hold values from -6 to 6
- owner_slot: int32 [128], replicated, may hold values from 0 to 127, as said below
- widths: int32 [128], replicated, may hold values from 90 to 360, as said below
- tap_weights: bfloat16 [128, 2880], replicated, may hold values from -0.21875 to 0.21875
Outputs:
- filtered: bfloat16 [128, 2880, 640], P('lat', 'lon')
Inputs may be any that keep to these rules, and one draw needn't show every extreme that they name: `owner_slot`: a permutation of the 128 rows; the 16 rows of each band of 16 rows are sent to every band of positions in equal numbers. `widths`: some row has the largest and some row the smallest value.
All inputs are finite; a program needn't handle non-finite values.
Results may differ from a plain program's by a relative error of at most 0.001.
Values may be sent and summed in bfloat16 or wider, within the bound.
A program may use at most 64 MiB of HBM per device.

v0:
```python
import jax
import jax.numpy as jnp
from jax import lax
from jax.sharding import PartitionSpec as P


def from_behind(x, axis, by):
    count = lax.axis_size(axis)
    return lax.ppermute(x, axis, [(i, (i + by) % count) for i in range(count)])


def body(fields, owner_slot, widths, tap_weights):
    lat_dev, lon_dev, channels = fields.shape
    n_lon = lax.axis_size("lon")
    n_lat = lax.axis_size("lat")
    circle = lon_dev * n_lon
    reach_dev = n_lon // 8
    my_band = lax.axis_index("lat")
    home_rows = my_band * lat_dev + jnp.arange(lat_dev, dtype=jnp.int32)
    dest_band = owner_slot // lat_dev
    ordering = jnp.argsort(dest_band[home_rows], stable=True)
    others = jnp.argsort((dest_band != my_band).astype(jnp.int32), stable=True)[:lat_dev]
    slot_of = owner_slot[others] % lat_dev
    placed = jnp.argsort(slot_of)
    owner_rows = others[placed]
    outgoing = fields[ordering].reshape(n_lat, lat_dev // n_lat, lon_dev, channels)
    incoming = lax.all_to_all(outgoing, "lat", split_axis=0, concat_axis=0, tiled=True)
    panel_rows = incoming.reshape(lat_dev, lon_dev, channels)[placed]
    offset = jnp.arange(circle, dtype=jnp.int32)
    distance = jnp.minimum(offset, circle - offset)
    active = jnp.where(
        distance[None, :] <= widths[owner_rows][:, None],
        tap_weights[owner_rows],
        jnp.zeros((), tap_weights.dtype),
    )
    columns = jnp.arange(lon_dev, dtype=jnp.int32)

    def sector_term(sector, sectors_off):
        tap_index = (sectors_off * lon_dev + columns[None, :] - columns[:, None]) % circle
        tap_block = jnp.take(active, tap_index, axis=1)
        return jnp.einsum("sim,smc->sic", tap_block, sector, preferred_element_type=jnp.float32)

    farthest = from_behind(panel_rows, "lon", -reach_dev)

    def advance(t, carry):
        summed, sector = carry
        sector = from_behind(sector, "lon", 1)
        return (summed + sector_term(sector, reach_dev - t), sector)

    summed = sector_term(farthest, reach_dev)
    summed, farthest = lax.fori_loop(1, 2 * reach_dev + 1, advance, (summed, farthest))
    return (panel_rows.astype(jnp.float32) + summed).astype(jnp.bfloat16)


def solution(mesh):
    in_specs = (P("lat", "lon", None), P(), P(), P())
    out_specs = P("lat", "lon", None)
    return jax.shard_map(body, mesh=mesh, in_specs=in_specs, out_specs=out_specs, check_vma=False)
```

profile of v0, /device:TPU:8, one launch (start us, length us, event | category | flops | bytes accessed | tf_op | source)
XLA Modules:
  0.0 931.0 jit_solution(17597640488246526952)
XLA Ops:
  7.9 9.3 all-to-all-start
  24.2 13.4 %all-to-all-done = bf16[8,2,45,640]{3,1,2,0:T(2,128)(2,1)S(1)} async-done(((bf16[8,2,45,640]{3,1,2,0:T(2,128)(2,1)}), bf16[8,2,45,640]{3,1,2,0:T(2,128)(2,1)S(1)}, u32[]{:S(2)}, u32[]{:S(2)}) %all-to-all-start) | async-done | bytes 921632 | tf_op jit(solution)/shard_map/all_to_all | solution.py:27
  38.7 9.2 collective-permute-start.1
  55.4 31.4 %collective-permute-done.1 = bf16[16,45,640]{2,0,1:T(8,128)(2,1)} collective-permute-done((bf16[16,45,640]{2,0,1:T(8,128)(2,1)S(1)}, bf16[16,45,640]{2,0,1:T(8,128)(2,1)}, u32[]{:S(2)}, u32[]{:S(2)}) %collective-permute-start.1) | collective-permute-done | bytes 921632 | tf_op jit(solution)/shard_map/ppermute | solution.py:9
  89.7 838.2 %while.19 = (s32[]{:T(128)}, f32[16,45,640]{2,1,0:T(8,128)}, bf16[16,45,640]{2,0,1:T(8,128)(2,1)}, bf16[16,2880]{0,1:T(8,128)(2,1)S(1)}, s32[]{:T(128)}, /*index=5*/s32[]{:T(128)}, s32[]{:T(128)}) while((s32[]{:T(128)}, f32[16,45,640]{2,1,0:T(8,128)}, bf16[16,45,640]{2,0,1:T(8,128)(2,1)}, ...), condition=%wide.region_4.6_spmd.clone.clone, body=%wide.region_3.5_spmd.clone.clone.sunk | while | flops 42013872 | bytes 10644627 | solution.py:51
  89.7 6.9 collective-permute-start
  103.6 34.0 %collective-permute-done = bf16[16,45,640]{2,0,1:T(8,128)(2,1)S(1)} collective-permute-done((bf16[16,45,640]{2,0,1:T(8,128)(2,1)}, bf16[16,45,640]{2,0,1:T(8,128)(2,1)S(1)}, u32[]{:S(2)}, u32[]{:S(2)}) %collective-permute-start) | collective-permute-done | bytes 921632 | tf_op jit(solution)/shard_map/while/body/eval_jaxpr/ppermute | solution.py:9
  150.8 41.7 %collective-permute-done = bf16[16,45,640]{2,0,1:T(8,128)(2,1)S(1)} collective-permute-done((bf16[16,45,640]{2,0,1:T(8,128)(2,1)}, bf16[16,45,640]{2,0,1:T(8,128)(2,1)S(1)}, u32[]{:S(2)}, u32[]{:S(2)}) %collective-permute-start) | collective-permute-done | bytes 921632 | tf_op jit(solution)/shard_map/while/body/eval_jaxpr/ppermute | solution.py:9
  205.6 40.5 %collective-permute-done = bf16[16,45,640]{2,0,1:T(8,128)(2,1)S(1)} collective-permute-done((bf16[16,45,640]{2,0,1:T(8,128)(2,1)}, bf16[16,45,640]{2,0,1:T(8,128)(2,1)S(1)}, u32[]{:S(2)}, u32[]{:S(2)}) %collective-permute-start) | collective-permute-done | bytes 921632 | tf_op jit(solution)/shard_map/while/body/eval_jaxpr/ppermute | solution.py:9
  259.3 50.6 %collective-permute-done = bf16[16,45,640]{2,0,1:T(8,128)(2,1)S(1)} collective-permute-done((bf16[16,45,640]{2,0,1:T(8,128)(2,1)}, bf16[16,45,640]{2,0,1:T(8,128)(2,1)S(1)}, u32[]{:S(2)}, u32[]{:S(2)}) %collective-permute-start) | collective-permute-done | bytes 921632 | tf_op jit(solution)/shard_map/while/body/eval_jaxpr/ppermute | solution.py:9
  314.1 8.2 collective-permute-start
  329.3 29.4 %collective-permute-done = bf16[16,45,640]{2,0,1:T(8,128)(2,1)S(1)} collective-permute-done((bf16[16,45,640]{2,0,1:T(8,128)(2,1)}, bf16[16,45,640]{2,0,1:T(8,128)(2,1)S(1)}, u32[]{:S(2)}, u32[]{:S(2)}) %collective-permute-start) | collective-permute-done | bytes 921632 | tf_op jit(solution)/shard_map/while/body/eval_jaxpr/ppermute | solution.py:9
  363.0 7.4 collective-permute-start
  377.4 34.5 %collective-permute-done = bf16[16,45,640]{2,0,1:T(8,128)(2,1)S(1)} collective-permute-done((bf16[16,45,640]{2,0,1:T(8,128)(2,1)}, bf16[16,45,640]{2,0,1:T(8,128)(2,1)S(1)}, u32[]{:S(2)}, u32[]{:S(2)}) %collective-permute-start) | collective-permute-done | bytes 921632 | tf_op jit(solution)/shard_map/while/body/eval_jaxpr/ppermute | solution.py:9
  425.0 42.3 %collective-permute-done = bf16[16,45,640]{2,0,1:T(8,128)(2,1)S(1)} collective-permute-done((bf16[16,45,640]{2,0,1:T(8,128)(2,1)}, bf16[16,45,640]{2,0,1:T(8,128)(2,1)S(1)}, u32[]{:S(2)}, u32[]{:S(2)}) %collective-permute-start) | collective-permute-done | bytes 921632 | tf_op jit(solution)/shard_map/while/body/eval_jaxpr/ppermute | solution.py:9
  480.5 35.2 %collective-permute-done = bf16[16,45,640]{2,0,1:T(8,128)(2,1)S(1)} collective-permute-done((bf16[16,45,640]{2,0,1:T(8,128)(2,1)}, bf16[16,45,640]{2,0,1:T(8,128)(2,1)S(1)}, u32[]{:S(2)}, u32[]{:S(2)}) %collective-permute-start) | collective-permute-done | bytes 921632 | tf_op jit(solution)/shard_map/while/body/eval_jaxpr/ppermute | solution.py:9
  532.3 40.1 %collective-permute-done = bf16[16,45,640]{2,0,1:T(8,128)(2,1)S(1)} collective-permute-done((bf16[16,45,640]{2,0,1:T(8,128)(2,1)}, bf16[16,45,640]{2,0,1:T(8,128)(2,1)S(1)}, u32[]{:S(2)}, u32[]{:S(2)}) %collective-permute-start) | collective-permute-done | bytes 921632 | tf_op jit(solution)/shard_map/while/body/eval_jaxpr/ppermute | solution.py:9
  585.6 58.2 %collective-permute-done = bf16[16,45,640]{2,0,1:T(8,128)(2,1)S(1)} collective-permute-done((bf16[16,45,640]{2,0,1:T(8,128)(2,1)}, bf16[16,45,640]{2,0,1:T(8,128)(2,1)S(1)}, u32[]{:S(2)}, u32[]{:S(2)}) %collective-permute-start) | collective-permute-done | bytes 921632 | tf_op jit(solution)/shard_map/while/body/eval_jaxpr/ppermute | solution.py:9
  656.9 43.3 %collective-permute-done = bf16[16,45,640]{2,0,1:T(8,128)(2,1)S(1)} collective-permute-done((bf16[16,45,640]{2,0,1:T(8,128)(2,1)}, bf16[16,45,640]{2,0,1:T(8,128)(2,1)S(1)}, u32[]{:S(2)}, u32[]{:S(2)}) %collective-permute-start) | collective-permute-done | bytes 921632 | tf_op jit(solution)/shard_map/while/body/eval_jaxpr/ppermute | solution.py:9
  713.4 42.3 %collective-permute-done = bf16[16,45,640]{2,0,1:T(8,128)(2,1)S(1)} collective-permute-done((bf16[16,45,640]{2,0,1:T(8,128)(2,1)}, bf16[16,45,640]{2,0,1:T(8,128)(2,1)S(1)}, u32[]{:S(2)}, u32[]{:S(2)}) %collective-permute-start) | collective-permute-done | bytes 921632 | tf_op jit(solution)/shard_map/while/body/eval_jaxpr/ppermute | solution.py:9
  768.9 41.4 %collective-permute-done = bf16[16,45,640]{2,0,1:T(8,128)(2,1)S(1)} collective-permute-done((bf16[16,45,640]{2,0,1:T(8,128)(2,1)}, bf16[16,45,640]{2,0,1:T(8,128)(2,1)S(1)}, u32[]{:S(2)}, u32[]{:S(2)}) %collective-permute-start) | collective-permute-done | bytes 921632 | tf_op jit(solution)/shard_map/while/body/eval_jaxpr/ppermute | solution.py:9
  823.5 38.4 %collective-permute-done = bf16[16,45,640]{2,0,1:T(8,128)(2,1)S(1)} collective-permute-done((bf16[16,45,640]{2,0,1:T(8,128)(2,1)}, bf16[16,45,640]{2,0,1:T(8,128)(2,1)S(1)}, u32[]{:S(2)}, u32[]{:S(2)}) %collective-permute-start) | collective-permute-done | bytes 921632 | tf_op jit(solution)/shard_map/while/body/eval_jaxpr/ppermute | solution.py:9
  875.1 20.7 %collective-permute-done = bf16[16,45,640]{2,0,1:T(8,128)(2,1)S(1)} collective-permute-done((bf16[16,45,640]{2,0,1:T(8,128)(2,1)}, bf16[16,45,640]{2,0,1:T(8,128)(2,1)S(1)}, u32[]{:S(2)}, u32[]{:S(2)}) %collective-permute-start) | collective-permute-done | bytes 921632 | tf_op jit(solution)/shard_map/while/body/eval_jaxpr/ppermute | solution.py:9
  909.0 14.7 %collective-permute-done = bf16[16,45,640]{2,0,1:T(8,128)(2,1)S(1)} collective-permute-done((bf16[16,45,640]{2,0,1:T(8,128)(2,1)}, bf16[16,45,640]{2,0,1:T(8,128)(2,1)S(1)}, u32[]{:S(2)}, u32[]{:S(2)}) %collective-permute-start) | collective-permute-done | bytes 921632 | tf_op jit(solution)/shard_map/while/body/eval_jaxpr/ppermute | solution.py:9
  (227 shorter events, 236.9 us)
Async XLA Ops:
  0.0 2.7 copy-start
  6.3 13.5 %copy-start.1 = (s32[128]{0:T(128)S(1)}, s32[128]{0:T(128)}, u32[]{:S(2)}) copy-start(s32[128]{0:T(128)} %param.9) | copy-start | bytes 1540
  6.3 14.2 %copy-start.4 = (bf16[128,2880]{0,1:T(8,128)(2,1)S(1)}, bf16[128,2880]{0,1:T(8,128)(2,1)}, u32[]{:S(2)}) copy-start(bf16[128,2880]{0,1:T(8,128)(2,1)} %param.11) | copy-start | bytes 2211844
  7.9 29.7 %all-to-all-start = ((bf16[8,2,45,640]{3,1,2,0:T(2,128)(2,1)}), bf16[8,2,45,640]{3,1,2,0:T(2,128)(2,1)S(1)}, u32[]{:S(2)}, u32[]{:S(2)}) async-start(bf16[8,2,45,640]{3,1,2,0:T(2,128)(2,1)} %copy.20), calls=%async_computation | async-start | bytes 1843200 | tf_op jit(solution)/shard_map/all_to_all | solution.py:27
  17.2 6.3 copy-start.2
  38.5 9.4 %copy-start.3 = (bf16[16,45,640]{2,1,0:T(8,128)(2,1)}, bf16[16,45,640]{2,1,0:T(8,128)(2,1)S(1)}, u32[]{:S(2)}) copy-start(bf16[16,45,640]{2,1,0:T(8,128)(2,1)S(1)} %gather_fusion.4) | copy-start | bytes 2764804
  38.7 48.2 %collective-permute-start.1 = (bf16[16,45,640]{2,0,1:T(8,128)(2,1)S(1)}, bf16[16,45,640]{2,0,1:T(8,128)(2,1)}, u32[]{:S(2)}, u32[]{:S(2)}) collective-permute-start(bf16[16,45,640]{2,0,1:T(8,128)(2,1)S(1)} %copy.25), channel_id=1, source_target_pairs={{0,448},{8,456},{16,464},{24,472},{32,480},{40,488},{48,496},{56,5... | collective-permute-start | bytes 2764808 | tf_op jit(solution)/shard_map/ppermute | solution.py:9
  89.7 47.9 %collective-permute-start = (bf16[16,45,640]{2,0,1:T(8,128)(2,1)}, bf16[16,45,640]{2,0,1:T(8,128)(2,1)S(1)}, u32[]{:S(2)}, u32[]{:S(2)}) collective-permute-start(bf16[16,45,640]{2,0,1:T(8,128)(2,1)} %get-tuple-element.231), channel_id=1, source_target_pairs={{0,8},{8,16},{16,24},{24,32},{32,40},{40,48},{48,56},{56,64},{64,7... | collective-permute-start | bytes 2764808 | tf_op jit(solution)/shard_map/while/body/eval_jaxpr/ppermute | solution.py:9
  141.8 50.6 %collective-permute-start = (bf16[16,45,640]{2,0,1:T(8,128)(2,1)}, bf16[16,45,640]{2,0,1:T(8,128)(2,1)S(1)}, u32[]{:S(2)}, u32[]{:S(2)}) collective-permute-start(bf16[16,45,640]{2,0,1:T(8,128)(2,1)} %get-tuple-element.231), channel_id=1, source_target_pairs={{0,8},{8,16},{16,24},{24,32},{32,40},{40,48},{48,56},{56,64},{64,7... | collective-permute-start | bytes 2764808 | tf_op jit(solution)/shard_map/while/body/eval_jaxpr/ppermute | solution.py:9
  196.7 49.4 %collective-permute-start = (bf16[16,45,640]{2,0,1:T(8,128)(2,1)}, bf16[16,45,640]{2,0,1:T(8,128)(2,1)S(1)}, u32[]{:S(2)}, u32[]{:S(2)}) collective-permute-start(bf16[16,45,640]{2,0,1:T(8,128)(2,1)} %get-tuple-element.231), channel_id=1, source_target_pairs={{0,8},{8,16},{16,24},{24,32},{32,40},{40,48},{48,56},{56,64},{64,7... | collective-permute-start | bytes 2764808 | tf_op jit(solution)/shard_map/while/body/eval_jaxpr/ppermute | solution.py:9
  250.3 59.5 %collective-permute-start = (bf16[16,45,640]{2,0,1:T(8,128)(2,1)}, bf16[16,45,640]{2,0,1:T(8,128)(2,1)S(1)}, u32[]{:S(2)}, u32[]{:S(2)}) collective-permute-start(bf16[16,45,640]{2,0,1:T(8,128)(2,1)} %get-tuple-element.231), channel_id=1, source_target_pairs={{0,8},{8,16},{16,24},{24,32},{32,40},{40,48},{48,56},{56,64},{64,7... | collective-permute-start | bytes 2764808 | tf_op jit(solution)/shard_map/while/body/eval_jaxpr/ppermute | solution.py:9
  314.1 44.6 %collective-permute-start = (bf16[16,45,640]{2,0,1:T(8,128)(2,1)}, bf16[16,45,640]{2,0,1:T(8,128)(2,1)S(1)}, u32[]{:S(2)}, u32[]{:S(2)}) collective-permute-start(bf16[16,45,640]{2,0,1:T(8,128)(2,1)} %get-tuple-element.231), channel_id=1, source_target_pairs={{0,8},{8,16},{16,24},{24,32},{32,40},{40,48},{48,56},{56,64},{64,7... | collective-permute-start | bytes 2764808 | tf_op jit(solution)/shard_map/while/body/eval_jaxpr/ppermute | solution.py:9
  363.0 48.9 %collective-permute-start = (bf16[16,45,640]{2,0,1:T(8,128)(2,1)}, bf16[16,45,640]{2,0,1:T(8,128)(2,1)S(1)}, u32[]{:S(2)}, u32[]{:S(2)}) collective-permute-start(bf16[16,45,640]{2,0,1:T(8,128)(2,1)} %get-tuple-element.231), channel_id=1, source_target_pairs={{0,8},{8,16},{16,24},{24,32},{32,40},{40,48},{48,56},{56,64},{64,7... | collective-permute-start | bytes 2764808 | tf_op jit(solution)/shard_map/while/body/eval_jaxpr/ppermute | solution.py:9
  416.1 51.2 %collective-permute-start = (bf16[16,45,640]{2,0,1:T(8,128)(2,1)}, bf16[16,45,640]{2,0,1:T(8,128)(2,1)S(1)}, u32[]{:S(2)}, u32[]{:S(2)}) collective-permute-start(bf16[16,45,640]{2,0,1:T(8,128)(2,1)} %get-tuple-element.231), channel_id=1, source_target_pairs={{0,8},{8,16},{16,24},{24,32},{32,40},{40,48},{48,56},{56,64},{64,7... | collective-permute-start | bytes 2764808 | tf_op jit(solution)/shard_map/while/body/eval_jaxpr/ppermute | solution.py:9
  471.6 44.2 %collective-permute-start = (bf16[16,45,640]{2,0,1:T(8,128)(2,1)}, bf16[16,45,640]{2,0,1:T(8,128)(2,1)S(1)}, u32[]{:S(2)}, u32[]{:S(2)}) collective-permute-start(bf16[16,45,640]{2,0,1:T(8,128)(2,1)} %get-tuple-element.231), channel_id=1, source_target_pairs={{0,8},{8,16},{16,24},{24,32},{32,40},{40,48},{48,56},{56,64},{64,7... | collective-permute-start | bytes 2764808 | tf_op jit(solution)/shard_map/while/body/eval_jaxpr/ppermute | solution.py:9
  520.0 52.4 %collective-permute-start = (bf16[16,45,640]{2,0,1:T(8,128)(2,1)}, bf16[16,45,640]{2,0,1:T(8,128)(2,1)S(1)}, u32[]{:S(2)}, u32[]{:S(2)}) collective-permute-start(bf16[16,45,640]{2,0,1:T(8,128)(2,1)} %get-tuple-element.231), channel_id=1, source_target_pairs={{0,8},{8,16},{16,24},{24,32},{32,40},{40,48},{48,56},{56,64},{64,7... | collective-permute-start | bytes 2764808 | tf_op jit(solution)/shard_map/while/body/eval_jaxpr/ppermute | solution.py:9
  576.7 67.1 %collective-permute-start = (bf16[16,45,640]{2,0,1:T(8,128)(2,1)}, bf16[16,45,640]{2,0,1:T(8,128)(2,1)S(1)}, u32[]{:S(2)}, u32[]{:S(2)}) collective-permute-start(bf16[16,45,640]{2,0,1:T(8,128)(2,1)} %get-tuple-element.231), channel_id=1, source_target_pairs={{0,8},{8,16},{16,24},{24,32},{32,40},{40,48},{48,56},{56,64},{64,7... | collective-permute-start | bytes 2764808 | tf_op jit(solution)/shard_map/while/body/eval_jaxpr/ppermute | solution.py:9
  648.0 52.2 %collective-permute-start = (bf16[16,45,640]{2,0,1:T(8,128)(2,1)}, bf16[16,45,640]{2,0,1:T(8,128)(2,1)S(1)}, u32[]{:S(2)}, u32[]{:S(2)}) collective-permute-start(bf16[16,45,640]{2,0,1:T(8,128)(2,1)} %get-tuple-element.231), channel_id=1, source_target_pairs={{0,8},{8,16},{16,24},{24,32},{32,40},{40,48},{48,56},{56,64},{64,7... | collective-permute-start | bytes 2764808 | tf_op jit(solution)/shard_map/while/body/eval_jaxpr/ppermute | solution.py:9
  704.5 51.3 %collective-permute-start = (bf16[16,45,640]{2,0,1:T(8,128)(2,1)}, bf16[16,45,640]{2,0,1:T(8,128)(2,1)S(1)}, u32[]{:S(2)}, u32[]{:S(2)}) collective-permute-start(bf16[16,45,640]{2,0,1:T(8,128)(2,1)} %get-tuple-element.231), channel_id=1, source_target_pairs={{0,8},{8,16},{16,24},{24,32},{32,40},{40,48},{48,56},{56,64},{64,7... | collective-permute-start | bytes 2764808 | tf_op jit(solution)/shard_map/while/body/eval_jaxpr/ppermute | solution.py:9
  760.0 50.3 %collective-permute-start = (bf16[16,45,640]{2,0,1:T(8,128)(2,1)}, bf16[16,45,640]{2,0,1:T(8,128)(2,1)S(1)}, u32[]{:S(2)}, u32[]{:S(2)}) collective-permute-start(bf16[16,45,640]{2,0,1:T(8,128)(2,1)} %get-tuple-element.231), channel_id=1, source_target_pairs={{0,8},{8,16},{16,24},{24,32},{32,40},{40,48},{48,56},{56,64},{64,7... | collective-permute-start | bytes 2764808 | tf_op jit(solution)/shard_map/while/body/eval_jaxpr/ppermute | solution.py:9
  814.6 47.3 %collective-permute-start = (bf16[16,45,640]{2,0,1:T(8,128)(2,1)}, bf16[16,45,640]{2,0,1:T(8,128)(2,1)S(1)}, u32[]{:S(2)}, u32[]{:S(2)}) collective-permute-start(bf16[16,45,640]{2,0,1:T(8,128)(2,1)} %get-tuple-element.231), channel_id=1, source_target_pairs={{0,8},{8,16},{16,24},{24,32},{32,40},{40,48},{48,56},{56,64},{64,7... | collective-permute-start | bytes 2764808 | tf_op jit(solution)/shard_map/while/body/eval_jaxpr/ppermute | solution.py:9
  866.1 29.7 %collective-permute-start = (bf16[16,45,640]{2,0,1:T(8,128)(2,1)}, bf16[16,45,640]{2,0,1:T(8,128)(2,1)S(1)}, u32[]{:S(2)}, u32[]{:S(2)}) collective-permute-start(bf16[16,45,640]{2,0,1:T(8,128)(2,1)} %get-tuple-element.231), channel_id=1, source_target_pairs={{0,8},{8,16},{16,24},{24,32},{32,40},{40,48},{48,56},{56,64},{64,7... | collective-permute-start | bytes 2764808 | tf_op jit(solution)/shard_map/while/body/eval_jaxpr/ppermute | solution.py:9
  900.1 23.7 %collective-permute-start = (bf16[16,45,640]{2,0,1:T(8,128)(2,1)}, bf16[16,45,640]{2,0,1:T(8,128)(2,1)S(1)}, u32[]{:S(2)}, u32[]{:S(2)}) collective-permute-start(bf16[16,45,640]{2,0,1:T(8,128)(2,1)} %get-tuple-element.231), channel_id=1, source_target_pairs={{0,8},{8,16},{16,24},{24,32},{32,40},{40,48},{48,56},{56,64},{64,7... | collective-permute-start | bytes 2764808 | tf_op jit(solution)/shard_map/while/body/eval_jaxpr/ppermute | solution.py:9
where the time goes:
time: 932 us; the launch traced here: 931 us
  waiting for transfers between devices  652 us (70%)
  local copies, waits for them, and re-layouts  144 us (15%)
  starting transfers between devices  69.1 us (7%)
  matrix products  55.7 us (6%)
    ppermute x17, waiting for transfers between devices, from_behind(): return lax.ppermute(x, axis, [(i, (i + by) % count) for i in range(count)])  639 us
    gather x51, local copies, waits for them, and re-layouts, sector_term(): tap_block = jnp.take(active, tap_index, axis=1)  115 us
    ppermute x17, starting transfers between devices, from_behind(): return lax.ppermute(x, axis, [(i, (i + by) % count) for i in range(count)])  59.8 us
    dot_general x17, matrix products, sector_term(): jnp.einsum('sim,smc->sic', tap_block, sector, preferred_element_type=jnp....  55.7 us
  transfers between devices with their start and end apart: 18, of which 18 were waited for; matrix products, arithmetic and copies ran while one was open for 14% of the time, Pallas kernels for 0%

commit v1 on v0

v1 whole, which is shorter than its diff:
```python
import jax
import jax.numpy as jnp
from jax import lax
from jax.experimental import pallas as pl
from jax.experimental.pallas import tpu as pltpu
from jax.sharding import PartitionSpec as P

MESH = pl.DeviceIdType.MESH

SECTOR = 45
PAD = 48
ROWS = 16
REACH = 360
CENTRE = 512
GROUP = 8
GROUP_K = GROUP + 16
CHUNKS = ((0, 640),)

BF16 = jnp.bfloat16
F32 = jnp.float32

ORDER = ((3, 0), (4, 0), (5, 1), (4, 1), (5, 0), (2, 0), (3, 1), (6, 1), (1, 0), (6, 0), (7, 1), (2, 1), (7, 0), (0, 0), (1, 1), (0, 1))


def div(a, b):
    return lax.div(a, jnp.int32(b))


def rem(a, b):
    return lax.rem(a, jnp.int32(b))


def device(x, z, y, c):
    return (x * 16 + z * 2 + div(y, 4), rem(y, 4) * 2 + c)


def job_of(z, y, c):
    shifted = rem(y + 6, 8)
    a, u = rem(shifted, 4), div(shifted, 4)
    return a, u, *destination(z, u, a, c)


def destination(z, u, a, c):
    b = rem(div(z, 2) + u + 2 * c + a, 4)
    to_core = rem(z + a, 2)
    return b, to_core


def kernel(owner, widths, fields, taps, out, *scratch):
    n = len(CHUNKS)
    per = [scratch[i * n:(i + 1) * n] for i in range(6)]
    outgoing, relay, window, done, back, landing = per
    toeplitz, tap_rows = scratch[6 * n:6 * n + 2]
    f1s, f1r, f2s, f2r, hs, hr, b1s, b1r, b2s, lr, tap_sem = scratch[6 * n + 2:]

    lon, lat = lax.axis_index("lon"), lax.axis_index("lat")
    x, z = div(lon, 16), rem(div(lon, 2), 8)
    y_hi, y_lo, c = rem(lon, 2), div(lat, 2), rem(lat, 2)
    y = y_hi * 4 + y_lo

    a, u, b, to_core = job_of(z, y, c)
    home = a * 2 + c

    tap_copy = pltpu.make_async_copy(taps.at[pl.ds(pl.multiple_of(home * ROWS, ROWS), ROWS), :], tap_rows, tap_sem)
    tap_copy.start()

    barrier = pltpu.get_barrier_semaphore()
    peers = 0
    for dy in range(8):
        for dc in range(2):
            if dy or dc:
                pl.semaphore_signal(barrier, inc=1, device_id=device(x, z, rem(y + dy, 8), rem(c + dc, 2)), device_id_type=MESH)
                peers += 1
    for dz in range(1, 8):
        pl.semaphore_signal(barrier, inc=1, device_id=device(x, rem(z + dz, 8), y, c), device_id_type=MESH)
        peers += 1
    for dx in (1, 3):
        pl.semaphore_signal(barrier, inc=1, device_id=device(rem(x + dx, 4), z, y, c), device_id_type=MESH)
        peers += 1

    to_band = [div(owner[lat * ROWS + j], ROWS) for j in range(ROWS)]
    code = []
    for j in range(ROWS):
        before = jnp.int32(0)
        for i in range(j):
            before = before + jnp.where(to_band[i] == to_band[j], 1, 0)
        code.append(to_band[j] * 2 + before)

    def stage(dz, side):
        to_z = rem(z + dz, 8)
        to_u = y_hi if side == 0 else 1 - y_hi
        to_b, core = destination(to_z, to_u, y_lo, c)
        wanted = (to_b * 2 + core) * 2 + to_u
        index = jnp.int32(0)
        for j in range(ROWS):
            index = index + jnp.where(code[j] == wanted, j, 0)
        t = dz * 2 + side
        index = jnp.minimum(index, ROWS - 1)
        for k, (lo, width) in enumerate(CHUNKS):
            outgoing[k][t, PAD - 16:, :] = jnp.zeros((16, width), BF16)
            outgoing[k][t, :SECTOR, :] = fields[index, :, lo:lo + width]

    def remote(src, dst, send, recv, dev):
        return pltpu.make_async_remote_copy(src_ref=src, dst_ref=dst, send_sem=send, recv_sem=recv, device_id=dev, device_id_type=MESH)

    sent = []

    def go(copy):
        copy.start()
        sent.append(copy)

    def y_to(side):
        return rem(y + (2 if side == 0 else 6), 8)

    def slot_of(src_z, src_y):
        return GROUP + src_z * 2 + div(src_y, 4)

    def forward_first(k, dz, side):
        t = dz * 2 + side
        src = outgoing[k].at[t]
        sem = k * 16 + t
        if dz == 0:
            go(remote(src, window[k].at[slot_of(z, y)], f2s.at[sem], f2r.at[sem], device(x, z, y_to(side), c)))
        elif dz % 2 == 0:
            go(remote(src, relay[k].at[t], f1s.at[sem], f1r.at[sem], device(x, z, y_to(side), c)))
        else:
            go(remote(src, relay[k].at[t], f1s.at[sem], f1r.at[sem], device(x, rem(z + dz, 8), y, c)))

    def forward_second(k, dz, side):
        if dz == 0:
            return
        t = dz * 2 + side
        sem = k * 16 + t
        here = relay[k].at[t]
        remote(here, here, f1s.at[sem], f1r.at[sem], device(x, z, y, c)).wait_recv()
        if dz % 2 == 0:
            src_y = rem(y + (6 if side == 0 else 2), 8)
            go(remote(here, window[k].at[slot_of(z, src_y)], f2s.at[sem], f2r.at[sem], device(x, rem(z + dz, 8), y, c)))
        else:
            src_z = rem(z + 8 - dz, 8)
            go(remote(here, window[k].at[slot_of(src_z, y)], f2s.at[sem], f2r.at[sem], device(x, z, y_to(side), c)))

    def halo(k, dz, side):
        t = dz * 2 + side
        sem = k * 16 + t
        src_z = rem(z + 8 - dz, 8)
        src_y = rem(y + (6 if side == 0 else 2), 8)
        slot = slot_of(src_z, src_y)
        here = window[k].at[slot]
        remote(here, here, f2s.at[sem], f2r.at[sem], device(x, z, y, c)).wait_recv()
        to_x = rem(x + 3 + 2 * div(src_z, 4), 4)
        go(remote(here, window[k].at[rem(slot + 16, 32)], hs.at[sem], hr.at[sem], device(to_x, z, y, c)))

    def halo_wait(k):
        for dz, side in ORDER:
            t = dz * 2 + side
            sem = k * 16 + t
            here = window[k].at[0]
            remote(here, here, hs.at[sem], hr.at[sem], device(x, z, y, c)).wait_recv()

    def toeplitz_of():
        tap_copy.wait()
        bands = [div(owner[home * ROWS + j], ROWS) for j in range(ROWS)]
        wanted = b * 2 + to_core
        seen, row = jnp.int32(0), jnp.int32(0)
        for j in range(ROWS):
            hit = jnp.where(bands[j] == wanted, 1, 0)
            row = row + jnp.where(seen == u, hit * j, 0)
            seen = seen + hit
        row = jnp.minimum(row, ROWS - 1)
        half = widths[home * ROWS + row]
        tap = tap_rows[...].astype(F32)
        pick = lax.broadcasted_iota(jnp.int32, tap.shape, 0) == row
        tap = jnp.sum(jnp.where(pick, tap, 0.0), axis=0, keepdims=True)
        tail = jnp.concatenate([tap[:, 2432:2880], jnp.zeros((1, 64), F32)], axis=1)
        tail = pltpu.roll(jnp.broadcast_to(tail, (8, 512)), 64, 1)[:1]
        line = jnp.concatenate([tail, tap[:, :512]], axis=1)
        offset = lax.broadcasted_iota(jnp.int32, line.shape, 1) - CENTRE
        line = jnp.where(jnp.abs(offset) <= half, line, 0.0)
        shifted = pltpu.roll(jnp.broadcast_to(line, (PAD, 1024)), 0, 1, stride=1, stride_axis=0)
        shifted = jnp.where(lax.broadcasted_iota(jnp.int32, shifted.shape, 0) < SECTOR, shifted, 0.0).astype(BF16)
        cols = GROUP_K * PAD
        col = lax.broadcasted_iota(jnp.int32, (1, cols), 1)
        sector = jnp.zeros_like(col)
        for d in range(1, GROUP_K):
            sector = sector + jnp.where(col >= PAD * d, 1, 0)
        within = col - sector * PAD
        source = jnp.where((within < SECTOR) & (sector < 17), sector * SECTOR + within + (CENTRE - REACH), -1)
        select = (lax.broadcasted_iota(jnp.int32, (1024, cols), 0) == source).astype(F32).astype(BF16)
        first = jnp.dot(shifted, select, preferred_element_type=F32)
        for s in range(GROUP):
            moved = first if s == 0 else pltpu.roll(first, PAD * s, 1)
            toeplitz[s * PAD:(s + 1) * PAD, :] = moved.astype(BF16)

    def compute(k):
        width = CHUNKS[k][1]
        for g in range(16 // GROUP):
            near = window[k][g * GROUP:g * GROUP + GROUP_K].reshape(GROUP_K * PAD, width)
            total = jnp.dot(toeplitz[...], near, preferred_element_type=F32)
            own = window[k][(g + 1) * GROUP:(g + 2) * GROUP].reshape(GROUP * PAD, width)
            total = own.astype(F32) + total
            done[k][g * GROUP:(g + 1) * GROUP] = total.astype(BF16).reshape(GROUP, PAD, width)

    unsent = []

    def here_or_there(src, dst, send, recv, to_y, core):
        stays = (to_y == y) & (core == c)
        copy = remote(src, dst, send, recv, device(x, z, to_y, core))

        @pl.when(stays)
        def _():
            pltpu.make_async_copy(src, dst, recv).start()

        @pl.when(jnp.logical_not(stays))
        def _():
            copy.start()

        unsent.append((stays, copy))

    def back_first(k, dz, side):
        sem = k * 16 + dz * 2 + side
        to_z = rem(z + dz, 8)
        here = done[k].at[to_z * 2 + side]
        if dz == 0:
            mine = home * 2 + u
            here_or_there(here, landing[k].at[mine], b1s.at[sem], lr.at[k * 16 + mine], b + 4 * side, to_core)
        elif dz % 2 == 0:
            place = 8 + div(a, 2) * 3 + dz // 2 - 1
            here_or_there(here, back[k].at[place], b1s.at[sem], b1r.at[k * 16 + place], b + 4 * side, to_core)
        else:
            place = side * 4 + dz // 2
            go(remote(here, back[k].at[place], b1s.at[sem], b1r.at[k * 16 + place], device(x, to_z, y, c)))

    def back_second(k, dz, side):
        if dz == 0:
            return
        sem = k * 16 + dz * 2 + side
        if dz % 2 == 0:
            place = 8 + side * 3 + dz // 2 - 1
            src_a = rem(c + z, 2) + 2 * side
            mix = rem(y_lo + 8 - div(z, 2) - src_a, 4)
            mine = (src_a * 2 + div(mix, 2)) * 2 + rem(mix, 2)
        else:
            place = side * 4 + dz // 2
            mine = home * 2 + u
        here = back[k].at[place]
        remote(here, here, b1s.at[sem], b1r.at[k * 16 + place], device(x, z, y, c)).wait_recv()
        there = landing[k].at[mine]
        arrived = lr.at[k * 16 + mine]
        if dz % 2 == 0:
            go(remote(here, there, b2s.at[sem], arrived, device(x, rem(z + dz, 8), y, c)))
        else:
            src_b, src_core = destination(rem(z + 8 - dz, 8), u, a, c)
            here_or_there(here, there, b2s.at[sem], arrived, src_b + 4 * side, src_core)

    def places():
        def add(band, found):
            found = list(found)
            seen = jnp.int32(0)
            for j in range(ROWS):
                at = owner[band * ROWS + j] - lat * ROWS
                for p in range(ROWS):
                    found[p] = found[p] + jnp.where(at == p, band * 2 + seen, 0)
                seen = seen + jnp.where((at >= 0) & (at < ROWS), 1, 0)
            return tuple(found)

        return lax.fori_loop(0, 8, add, (jnp.int32(0),) * ROWS)

    for dz, side in ORDER:
        stage(dz, side)
    pl.semaphore_wait(barrier, peers)
    for k in range(n):
        for dz, side in ORDER:
            forward_first(k, dz, side)
    toeplitz_of()
    for k in range(n):
        for dz, side in ORDER:
            forward_second(k, dz, side)
    found = places()
    for k in range(n):
        for dz, side in ORDER:
            halo(k, dz, side)
    for k in range(n):
        halo_wait(k)
        compute(k)
        for dz, side in ORDER:
            back_first(k, dz, side)
    for k in range(n):
        for dz, side in ORDER:
            back_second(k, dz, side)
    for k, (lo, width) in enumerate(CHUNKS):
        for mine in range(ROWS):
            here = landing[k].at[mine]
            remote(here, here, b2s.at[0], lr.at[k * 16 + mine], device(x, z, y, c)).wait_recv()
        for p in range(ROWS):
            out[p, :, lo:lo + width] = landing[k][jnp.minimum(found[p], ROWS - 1), :SECTOR, :]
    for copy in sent:
        copy.wait_send()
    for stays, copy in unsent:

        @pl.when(jnp.logical_not(stays))
        def _(copy=copy):
            copy.wait_send()


def body(fields, owner_slot, widths, tap_weights):
    n = len(CHUNKS)
    buffers = []
    for slots in (16, 16, 32, 16, 16, 16):
        buffers += [pltpu.VMEM((slots, PAD, width), BF16) for _, width in CHUNKS]
    return pl.pallas_call(
        kernel,
        out_shape=jax.ShapeDtypeStruct(fields.shape, BF16),
        in_specs=[
            pl.BlockSpec(memory_space=pltpu.SMEM),
            pl.BlockSpec(memory_space=pltpu.SMEM),
            pl.BlockSpec(memory_space=pltpu.VMEM),
            pl.BlockSpec(memory_space=pl.ANY),
        ],
        out_specs=pl.BlockSpec(memory_space=pltpu.VMEM),
        scratch_shapes=[
            *buffers,
            pltpu.VMEM((GROUP * PAD, GROUP_K * PAD), BF16),
            pltpu.VMEM((ROWS, tap_weights.shape[1]), BF16),
            *[pltpu.SemaphoreType.DMA((n * 16,)) for _ in range(10)],
            pltpu.SemaphoreType.DMA,
        ],
        compiler_params=pltpu.CompilerParams(collective_id=0, has_side_effects=True, vmem_limit_bytes=40 << 20),
    )(owner_slot, widths, fields, tap_weights)


def solution(mesh):
    in_specs = (P("lat", "lon", None), P(), P(), P())
    out_specs = P("lat", "lon", None)
    return jax.shard_map(body, mesh=mesh, in_specs=in_specs, out_specs=out_specs, check_vma=False)
```

time: 932 us -> 79.1 us (0.08)
  the two profiles are of different devices: /device:TPU:8 before, /device:TPU:1 now
where the time goes in v1:
time: 79.1 us; the launch traced here: 78.3 us
  Pallas kernels  74.9 us (95%)
  local copies, waits for them, and re-layouts  3.29 us (4%)
    pallas_call x1, Pallas kernels, body(): pl.pallas_call(kernel, out_shape=jax.ShapeDtypeStruct(fields.shape, BF16)...  74.9 us
    unnamed x8, local copies, waits for them, and re-layouts  2.19 us

profile of v1, /device:TPU:1, one launch (start us, length us, event | category | flops | bytes accessed | tf_op | source)
XLA Modules:
  0.0 78.3 jit_solution(17377350387360382569)
XLA Ops:
  0.0 0.0 copy-start.2
  0.0 1.5 %copy.6.taps = bf16[128,2880]{1,0:T(8,128)(2,1)S(1)} copy(bf16[128,2880]{0,1:T(8,128)(2,1)} %param.7) | data formatting | bytes 1474560 | tf_op args[3]
  1.5 0.0 copy-done.2
  1.6 0.0 copy-start
  1.6 0.0 copy-start.1
  1.6 0.2 copy.5.fields
  1.8 0.4 copy-done
  2.2 0.0 copy-done.1
  2.2 74.9 %shard_map.46 = bf16[16,45,640]{2,1,0:T(8,128)(2,1)S(1)} custom-call(s32[128]{0:T(128)S(1)} %copy-done, s32[128]{0:T(128)S(1)} %copy-done.1, bf16[16,45,640]{2,1,0:T(8,128)(2,1)S(1)} %copy.5.fields, bf16[128,2880]{1,0:T(8,128)(2,1)S(1)} %copy.6.taps), custom_call_target="tpu_custom_call" | custom-call | tf_op jit(solution)/shard_map/pallas_call | solution.py:311
  77.2 1.1 %copy.7 = bf16[16,45,640]{2,0,1:T(8,128)(2,1)} copy(bf16[16,45,640]{2,1,0:T(8,128)(2,1)S(1)} %shard_map.46) | data formatting | bytes 1843200 | tf_op jit(solution)/shard_map/pallas_call | solution.py:311
Async XLA Ops:
  0.0 1.5 %copy-start.2 = (bf16[16,45,640]{2,0,1:T(8,128)(2,1)S(1)}, bf16[16,45,640]{2,0,1:T(8,128)(2,1)}, u32[]{:S(2)}) copy-start(bf16[16,45,640]{2,0,1:T(8,128)(2,1)} %param.4) | copy-start | bytes 2764804
  1.6 0.7 copy-start
  1.6 0.7 copy-start.1

commit v2 on v1

--- a/solution.py
+++ b/solution.py
@@ -14,20 +14,23 @@
 CENTRE = 512
 GROUP = 8
 GROUP_K = GROUP + 16
-CHUNKS = ((0, 640),)
+CHUNKS = ((0, 384), (384, 256),)
+
+
+ORDER = ((1, 0), (4, 1), (7, 1), (4, 0), (3, 1), (5, 0), (0, 0), (0, 1), (1, 1), (7, 0), (6, 1), (2, 1), (6, 0), (2, 0), (5, 1), (3, 0))
+
+STEPS = {"A": "first", "R": "second", "H": "halo", "C": "filter", "S": "back", "F": "finish", "W": "weights", "P": "places"}
+PLAN = ("A0.0", "W", "A0.1", "R0.0", "R0.1", "A1.1", "H0.0", "P", "A1.0", "H0.1", "R1.1", "R1.0", "C0", "H1.1", "H1.0", "S0.0", "C1", "S0.1", "S1.0", "S1.1", "F0", "F1")
 
 BF16 = jnp.bfloat16
 F32 = jnp.float32
 
-ORDER = ((3, 0), (4, 0), (5, 1), (4, 1), (5, 0), (2, 0), (3, 1), (6, 1), (1, 0), (6, 0), (7, 1), (2, 1), (7, 0), (0, 0), (1, 1), (0, 1))
-
-
 def div(a, b):
-    return lax.div(a, jnp.int32(b))
+    return lax.shift_right_logical(a, jnp.int32(b.bit_length() - 1))
 
 
 def rem(a, b):
-    return lax.rem(a, jnp.int32(b))
+    return lax.bitwise_and(a, jnp.int32(b - 1))
 
 
 def device(x, z, y, c):
@@ -46,37 +49,43 @@
     return b, to_core
 
 
-def kernel(owner, widths, fields, taps, out, *scratch):
+def kernel(owner_in, widths_in, fields_in, taps, out, *scratch):
     n = len(CHUNKS)
     per = [scratch[i * n:(i + 1) * n] for i in range(6)]
     outgoing, relay, window, done, back, landing = per
-    toeplitz, tap_rows = scratch[6 * n:6 * n + 2]
-    f1s, f1r, f2s, f2r, hs, hr, b1s, b1r, b2s, lr, tap_sem = scratch[6 * n + 2:]
+    toeplitz, tap_rows, by_column, fields = scratch[6 * n:6 * n + 4]
+    owner, widths, f1s, f1r, f2s, f2r, hs, hr, b1s, b1r, b2s, lr, tap_sem, owner_sem, width_sem, field_sem = scratch[6 * n + 4:]
 
     lon, lat = lax.axis_index("lon"), lax.axis_index("lat")
     x, z = div(lon, 16), rem(div(lon, 2), 8)
     y_hi, y_lo, c = rem(lon, 2), div(lat, 2), rem(lat, 2)
     y = y_hi * 4 + y_lo
 
+    barrier = pltpu.get_barrier_semaphore()
+    greeted = [device(x, rem(z + dz, 8), y, c) for dz in (4, 3, 5)]
+    greeted += [device(x, z, rem(y + dy, 8), rem(c + dc, 2)) for dy in (4, 3, 5) for dc in range(2)]
+    greeted += [device(x, rem(z + dz, 8), y, c) for dz in (2, 6)]
+    greeted += [device(x, z, rem(y + dy, 8), rem(c + dc, 2)) for dy in (2, 6, 1, 7) for dc in range(2)]
+    greeted += [device(x, rem(z + dz, 8), y, c) for dz in (1, 7)]
+    greeted += [device(rem(x + dx, 4), z, y, c) for dx in (1, 3)] + [device(x, z, y, 1 - c)]
+    for each in greeted:
+        pl.semaphore_signal(barrier, inc=1, device_id=each, device_id_type=MESH)
+    peers = len(greeted)
+
     a, u, b, to_core = job_of(z, y, c)
     home = a * 2 + c
 
-    tap_copy = pltpu.make_async_copy(taps.at[pl.ds(pl.multiple_of(home * ROWS, ROWS), ROWS), :], tap_rows, tap_sem)
+    field_copies = [pltpu.make_async_copy(fields_in.at[pl.ds(i * 9, 9)], by_column.at[pl.ds(i * 9, 9)], field_sem.at[i]) for i in range(5)]
+    tap_copy = pltpu.make_async_copy(taps, tap_rows, tap_sem)
+    owner_copy = pltpu.make_async_copy(owner_in, owner, owner_sem)
+    owner_copy.start()
+    width_copy = pltpu.make_async_copy(widths_in, widths, width_sem)
+    width_copy.start()
+    for copy in field_copies:
+        copy.start()
+
     tap_copy.start()
-
-    barrier = pltpu.get_barrier_semaphore()
-    peers = 0
-    for dy in range(8):
-        for dc in range(2):
-            if dy or dc:
-                pl.semaphore_signal(barrier, inc=1, device_id=device(x, z, rem(y + dy, 8), rem(c + dc, 2)), device_id_type=MESH)
-                peers += 1
-    for dz in range(1, 8):
-        pl.semaphore_signal(barrier, inc=1, device_id=device(x, rem(z + dz, 8), y, c), device_id_type=MESH)
-        peers += 1
-    for dx in (1, 3):
-        pl.semaphore_signal(barrier, inc=1, device_id=device(rem(x + dx, 4), z, y, c), device_id_type=MESH)
-        peers += 1
+    owner_copy.wait()
 
     to_band = [div(owner[lat * ROWS + j], ROWS) for j in range(ROWS)]
     code = []
@@ -98,7 +107,7 @@
         index = jnp.minimum(index, ROWS - 1)
         for k, (lo, width) in enumerate(CHUNKS):
             outgoing[k][t, PAD - 16:, :] = jnp.zeros((16, width), BF16)
-            outgoing[k][t, :SECTOR, :] = fields[index, :, lo:lo + width]
+            outgoing[k][t, :SECTOR, :] = fields[index, :SECTOR, lo:lo + width]
 
     def remote(src, dst, send, recv, dev):
         return pltpu.make_async_remote_copy(src_ref=src, dst_ref=dst, send_sem=send, recv_sem=recv, device_id=dev, device_id_type=MESH)
@@ -160,6 +169,7 @@
 
     def toeplitz_of():
         tap_copy.wait()
+        width_copy.wait()
         bands = [div(owner[home * ROWS + j], ROWS) for j in range(ROWS)]
         wanted = b * 2 + to_core
         seen, row = jnp.int32(0), jnp.int32(0)
@@ -169,25 +179,27 @@
             seen = seen + hit
         row = jnp.minimum(row, ROWS - 1)
         half = widths[home * ROWS + row]
-        tap = tap_rows[...].astype(F32)
-        pick = lax.broadcasted_iota(jnp.int32, tap.shape, 0) == row
-        tap = jnp.sum(jnp.where(pick, tap, 0.0), axis=0, keepdims=True)
+        pick = (lax.broadcasted_iota(jnp.int32, (8, 128), 1) == home * ROWS + row).astype(F32).astype(BF16)
+        tap = lax.dot_general(pick, tap_rows[...], (((1,), (1,)), ((), ())), preferred_element_type=F32)[:1]
         tail = jnp.concatenate([tap[:, 2432:2880], jnp.zeros((1, 64), F32)], axis=1)
         tail = pltpu.roll(jnp.broadcast_to(tail, (8, 512)), 64, 1)[:1]
         line = jnp.concatenate([tail, tap[:, :512]], axis=1)
         offset = lax.broadcasted_iota(jnp.int32, line.shape, 1) - CENTRE
         line = jnp.where(jnp.abs(offset) <= half, line, 0.0)
         shifted = pltpu.roll(jnp.broadcast_to(line, (PAD, 1024)), 0, 1, stride=1, stride_axis=0)
-        shifted = jnp.where(lax.broadcasted_iota(jnp.int32, shifted.shape, 0) < SECTOR, shifted, 0.0).astype(BF16)
-        cols = GROUP_K * PAD
-        col = lax.broadcasted_iota(jnp.int32, (1, cols), 1)
-        sector = jnp.zeros_like(col)
-        for d in range(1, GROUP_K):
-            sector = sector + jnp.where(col >= PAD * d, 1, 0)
-        within = col - sector * PAD
-        source = jnp.where((within < SECTOR) & (sector < 17), sector * SECTOR + within + (CENTRE - REACH), -1)
-        select = (lax.broadcasted_iota(jnp.int32, (1024, cols), 0) == source).astype(F32).astype(BF16)
-        first = jnp.dot(shifted, select, preferred_element_type=F32)
+        shifted = jnp.where(lax.broadcasted_iota(jnp.int32, shifted.shape, 0) < SECTOR, shifted, 0.0)
+        lane = lax.broadcasted_iota(jnp.int32, (PAD, 256), 1)
+        columns = [jnp.zeros((PAD, 128), F32) for _ in range(GROUP_K * PAD // 128)]
+        for d in range(17):
+            old, new = CENTRE - REACH + SECTOR * d, PAD * d
+            old_tile, new_tile = old // 128, new // 128
+            old, new = old % 128, new % 128
+            moved = pltpu.roll(shifted[:, old_tile * 128:old_tile * 128 + 256], (new - old) % 256, 1)
+            moved = jnp.where((lane >= new) & (lane < new + SECTOR), moved, 0.0)
+            columns[new_tile] = columns[new_tile] + moved[:, :128]
+            if new + SECTOR > 128:
+                columns[new_tile + 1] = columns[new_tile + 1] + moved[:, 128:]
+        first = jnp.concatenate(columns, axis=1)
         for s in range(GROUP):
             moved = first if s == 0 else pltpu.roll(first, PAD * s, 1)
             toeplitz[s * PAD:(s + 1) * PAD, :] = moved.astype(BF16)
@@ -254,46 +266,67 @@
             here_or_there(here, there, b2s.at[sem], arrived, src_b + 4 * side, src_core)
 
     def places():
-        def add(band, found):
-            found = list(found)
+        slots = []
+        for band in range(8):
             seen = jnp.int32(0)
+            pair = [jnp.int32(0), jnp.int32(0)]
             for j in range(ROWS):
                 at = owner[band * ROWS + j] - lat * ROWS
-                for p in range(ROWS):
-                    found[p] = found[p] + jnp.where(at == p, band * 2 + seen, 0)
-                seen = seen + jnp.where((at >= 0) & (at < ROWS), 1, 0)
-            return tuple(found)
-
-        return lax.fori_loop(0, 8, add, (jnp.int32(0),) * ROWS)
-
-    for dz, side in ORDER:
-        stage(dz, side)
-    pl.semaphore_wait(barrier, peers)
-    for k in range(n):
-        for dz, side in ORDER:
-            forward_first(k, dz, side)
-    toeplitz_of()
-    for k in range(n):
-        for dz, side in ORDER:
-            forward_second(k, dz, side)
-    found = places()
-    for k in range(n):
-        for dz, side in ORDER:
-            halo(k, dz, side)
-    for k in range(n):
+                mine = (at >= 0) & (at < ROWS)
+                for r in range(2):
+                    pair[r] = pair[r] + jnp.where(mine & (seen == r), at, 0)
+                seen = seen + jnp.where(mine, 1, 0)
+            slots += pair
+        found = []
+        for p in range(ROWS):
+            place = jnp.int32(0)
+            for mine, slot in enumerate(slots):
+                place = place + jnp.where(slot == p, mine, 0)
+            found.append(jnp.minimum(place, ROWS - 1))
+        return found
+
+    found = [None]
+
+    def filter_chunk(k):
         halo_wait(k)
         compute(k)
         for dz, side in ORDER:
             back_first(k, dz, side)
-    for k in range(n):
-        for dz, side in ORDER:
-            back_second(k, dz, side)
-    for k, (lo, width) in enumerate(CHUNKS):
+
+    def finish(k):
+        lo, width = CHUNKS[k]
         for mine in range(ROWS):
             here = landing[k].at[mine]
             remote(here, here, b2s.at[0], lr.at[k * 16 + mine], device(x, z, y, c)).wait_recv()
         for p in range(ROWS):
-            out[p, :, lo:lo + width] = landing[k][jnp.minimum(found[p], ROWS - 1), :SECTOR, :]
+            out[p, :, lo:lo + width] = landing[k][found[0][p], :SECTOR, :]
+
+    parts = {"first": forward_first, "second": forward_second, "halo": halo, "back": back_second}
+    whole = {"filter": filter_chunk, "finish": finish}
+
+    for copy in field_copies:
+        copy.wait()
+    fields[:, :SECTOR, :] = jnp.swapaxes(by_column[...], 0, 1)
+    staged = [ORDER[0]]
+    stage(*ORDER[0])
+    pl.semaphore_wait(barrier, peers)
+    for token in PLAN:
+        name = STEPS[token[0]]
+        if name == "weights":
+            toeplitz_of()
+        elif name == "places":
+            found[0] = places()
+        elif name in whole:
+            whole[name](int(token[1]))
+        else:
+            start = 8 if token.endswith(".1") else 0
+            stop = 8 if token.endswith(".0") else 16
+            for message in ORDER[start:stop]:
+                if message not in staged:
+                    staged.append(message)
+                    stage(*message)
+                parts[name](int(token[1]), *message)
+
     for copy in sent:
         copy.wait_send()
     for stays, copy in unsent:
@@ -312,21 +345,26 @@
         kernel,
         out_shape=jax.ShapeDtypeStruct(fields.shape, BF16),
         in_specs=[
-            pl.BlockSpec(memory_space=pltpu.SMEM),
-            pl.BlockSpec(memory_space=pltpu.SMEM),
-            pl.BlockSpec(memory_space=pltpu.VMEM),
-            pl.BlockSpec(memory_space=pl.ANY),
+            pl.BlockSpec(memory_space=pltpu.HBM),
+            pl.BlockSpec(memory_space=pltpu.HBM),
+            pl.BlockSpec(memory_space=pltpu.HBM),
+            pl.BlockSpec(memory_space=pltpu.HBM),
         ],
         out_specs=pl.BlockSpec(memory_space=pltpu.VMEM),
         scratch_shapes=[
             *buffers,
             pltpu.VMEM((GROUP * PAD, GROUP_K * PAD), BF16),
-            pltpu.VMEM((ROWS, tap_weights.shape[1]), BF16),
+            pltpu.VMEM(tap_weights.shape[::-1], BF16),
+            pltpu.VMEM((SECTOR, ROWS, fields.shape[2]), BF16),
+            pltpu.VMEM((ROWS, PAD, fields.shape[2]), BF16),
+            pltpu.SMEM(owner_slot.shape, jnp.int32),
+            pltpu.SMEM(widths.shape, jnp.int32),
             *[pltpu.SemaphoreType.DMA((n * 16,)) for _ in range(10)],
-            pltpu.SemaphoreType.DMA,
+            *[pltpu.SemaphoreType.DMA for _ in range(3)],
+            pltpu.SemaphoreType.DMA((5,)),
         ],
         compiler_params=pltpu.CompilerParams(collective_id=0, has_side_effects=True, vmem_limit_bytes=40 << 20),
-    )(owner_slot, widths, fields, tap_weights)
+    )(*[pltpu.with_memory_space_constraint(each, pltpu.HBM) for each in (owner_slot, widths, jnp.swapaxes(fields, 0, 1), tap_weights.T)])
 
 
 def solution(mesh):

time: 79.1 us -> 66.3 us (0.84)
  Pallas kernels: 74.9 us -> 65.1 us
  local copies, waits for them, and re-layouts: 3.29 us -> 1.1 us
    pallas_call x1, Pallas kernels: 74.9 us -> 65.1 us  [body(): pl.pallas_call(kernel, out_shape=jax.ShapeDtypeStruct(fields.shape, BF16)...]
    unnamed x8 -> x0, local copies, waits for them, and re-layouts: 2.19 us -> none
where the time goes in v2:
time: 66.3 us; the launch traced here: 66.2 us
  Pallas kernels  65.1 us (98%)
  local copies, waits for them, and re-layouts  1.1 us (2%)
    pallas_call x1, Pallas kernels, body(): pl.pallas_call(kernel, out_shape=jax.ShapeDtypeStruct(fields.shape, BF16)...  65.1 us

profile of v2, /device:TPU:1, one launch (start us, length us, event | category | flops | bytes accessed | tf_op | source)
XLA Modules:
  0.0 66.2 jit_solution(8888554891014191299)
XLA Ops:
  0.0 65.1 %shard_map.46 = bf16[16,45,640]{2,1,0:T(8,128)(2,1)S(1)} custom-call(s32[128]{0:T(128)} %owner_in.1, s32[128]{0:T(128)} %widths_in.1, bf16[45,16,640]{2,1,0:T(8,128)(2,1)} %bitcast.2, bf16[2880,128]{1,0:T(8,128)(2,1)} %bitcast.3), custom_call_target="tpu_custom_call" | custom-call | tf_op jit(solution)/shard_map/pallas_call | solution.py:344
  65.1 1.1 %copy.5 = bf16[16,45,640]{2,0,1:T(8,128)(2,1)} copy(bf16[16,45,640]{2,1,0:T(8,128)(2,1)S(1)} %shard_map.46) | data formatting | bytes 1843200 | tf_op jit(solution)/shard_map/pallas_call | solution.py:344

commit v3 on v2

--- a/solution.py
+++ b/solution.py
@@ -19,8 +19,8 @@
 
 ORDER = ((1, 0), (4, 1), (7, 1), (4, 0), (3, 1), (5, 0), (0, 0), (0, 1), (1, 1), (7, 0), (6, 1), (2, 1), (6, 0), (2, 0), (5, 1), (3, 0))
 
-STEPS = {"A": "first", "R": "second", "H": "halo", "C": "filter", "S": "back", "F": "finish", "W": "weights", "P": "places"}
-PLAN = ("A0.0", "W", "A0.1", "R0.0", "R0.1", "A1.1", "H0.0", "P", "A1.0", "H0.1", "R1.1", "R1.0", "C0", "H1.1", "H1.0", "S0.0", "C1", "S0.1", "S1.0", "S1.1", "F0", "F1")
+STEPS = {"A": "first", "R": "second", "H": "halo", "C": "filter", "S": "back", "F": "finish", "W": "weights", "P": "places", "D": "drain"}
+PLAN = ("A0.0", "W", "A0.1", "R0.0", "R0.1", "A1.1", "H0.0", "P", "A1.0", "H0.1", "R1.1", "R1.0", "C0", "H1.1", "H1.0", "S0.0", "C1", "S0.1", "S1.0", "S1.1", "D0", "F0", "F1")
 
 BF16 = jnp.bfloat16
 F32 = jnp.float32
@@ -116,7 +116,7 @@
 
     def go(copy):
         copy.start()
-        sent.append(copy)
+        sent.append((None, copy))
 
     def y_to(side):
         return rem(y + (2 if side == 0 else 6), 8)
@@ -213,8 +213,6 @@
             total = own.astype(F32) + total
             done[k][g * GROUP:(g + 1) * GROUP] = total.astype(BF16).reshape(GROUP, PAD, width)
 
-    unsent = []
-
     def here_or_there(src, dst, send, recv, to_y, core):
         stays = (to_y == y) & (core == c)
         copy = remote(src, dst, send, recv, device(x, z, to_y, core))
@@ -227,7 +225,7 @@
         def _():
             copy.start()
 
-        unsent.append((stays, copy))
+        sent.append((stays, copy))
 
     def back_first(k, dz, side):
         sem = k * 16 + dz * 2 + side
@@ -304,6 +302,18 @@
     parts = {"first": forward_first, "second": forward_second, "halo": halo, "back": back_second}
     whole = {"filter": filter_chunk, "finish": finish}
 
+    def drain(keep):
+        while len(sent) > keep:
+            stays, copy = sent.pop(0)
+            if stays is None:
+                copy.wait_send()
+            else:
+
+                @pl.when(jnp.logical_not(stays))
+                def _(copy=copy):
+                    copy.wait_send()
+
+
     for copy in field_copies:
         copy.wait()
     fields[:, :SECTOR, :] = jnp.swapaxes(by_column[...], 0, 1)
@@ -316,6 +326,8 @@
             toeplitz_of()
         elif name == "places":
             found[0] = places()
+        elif name == "drain":
+            drain(int(token[1:]))
         elif name in whole:
             whole[name](int(token[1]))
         else:
@@ -326,14 +338,7 @@
                     staged.append(message)
                     stage(*message)
                 parts[name](int(token[1]), *message)
-
-    for copy in sent:
-        copy.wait_send()
-    for stays, copy in unsent:
-
-        @pl.when(jnp.logical_not(stays))
-        def _(copy=copy):
-            copy.wait_send()
+    drain(0)
 
 
 def body(fields, owner_slot, widths, tap_weights):

time: 66.3 us -> 65.8 us (level)
  Pallas kernels: 65.1 us -> 64.4 us
    pallas_call x1, Pallas kernels: 65.1 us -> 64.4 us  [body(): pl.pallas_call(kernel, out_shape=jax.ShapeDtypeStruct(fields.shape, BF16)...]
where the time goes in v3:
time: 65.8 us; the launch traced here: 65.5 us
  Pallas kernels  64.4 us (98%)
  local copies, waits for them, and re-layouts  1.1 us (2%)
    pallas_call x1, Pallas kernels, body(): pl.pallas_call(kernel, out_shape=jax.ShapeDtypeStruct(fields.shape, BF16)...  64.4 us

profile of v3, /device:TPU:1, one launch (start us, length us, event | category | flops | bytes accessed | tf_op | source)
XLA Modules:
  0.0 65.5 jit_solution(5863476143908858598)
XLA Ops:
  0.0 64.4 %shard_map.46 = bf16[16,45,640]{2,1,0:T(8,128)(2,1)S(1)} custom-call(s32[128]{0:T(128)} %owner_in.1, s32[128]{0:T(128)} %widths_in.1, bf16[45,16,640]{2,1,0:T(8,128)(2,1)} %bitcast.2, bf16[2880,128]{1,0:T(8,128)(2,1)} %bitcast.3), custom_call_target="tpu_custom_call" | custom-call | tf_op jit(solution)/shard_map/pallas_call | solution.py:349
  64.4 1.1 %copy.5 = bf16[16,45,640]{2,0,1:T(8,128)(2,1)} copy(bf16[16,45,640]{2,1,0:T(8,128)(2,1)S(1)} %shard_map.46) | data formatting | bytes 1843200 | tf_op jit(solution)/shard_map/pallas_call | solution.py:349
